TPU v7x, 512 devices: a whole 4x8x8 slice. The times are simulated.
512 devices in a mesh: ctx: 64 (over y_lo, z, core), head: 8 (over x, y_hi).
Axes of the slice: x: 4, y: 8 (y_hi: 2, y_lo: 4; y = y_hi * 4 + y_lo), z: 8, core: 2. Of those that a mesh axis runs over, the one named last changes fastest.
Arguments:
- queries: bfloat16 [8192, 8192], P('ctx', 'head'), may hold values from -8 to 8
- key_vector_rows: bfloat16 [8192, 1024], P('ctx', 'head'), may hold values from -8 to 8
- values: bfloat16 [8192, 1024], P('ctx', 'head'), may hold values from -6 to 6
- doc_lengths: int32 [128], replicated, may hold values from 1 to 4224, 8192 in all
Outputs:
- attended: bfloat16 [8192, 8192], P(('ctx', 'head'))
Inputs may be any that keep to these rules, and one draw needn't show every extreme that they name: `doc_lengths`: the 128 lengths sum to 8192, and one of them is exactly 4224.
All inputs are finite; a program needn't handle non-finite values.
Results may differ from a plain program's by a relative error of at most 0.0025.
Values may be sent and summed in bfloat16 or wider, within the bound.
A program may use at most 64 MiB of HBM per device.

v0:
```python
import math
import jax
import jax.numpy as jnp
from jax import lax
from jax.sharding import PartitionSpec as P

HEAD_SIZE = 128


def doc_numbers(doc_ends, positions):
    return jnp.sum((doc_ends[None, :] <= positions[:, None]).astype(jnp.int32), axis=1)


def attend(running, block_of_keys, block_of_values, key_pos, query_info):
    query_heads, query_pos, query_docs, doc_ends = query_info
    key_docs = doc_numbers(doc_ends, key_pos)
    allowed = (
        (key_docs[None, :] == query_docs[:, None])
        & (key_pos[None, :] <= query_pos[:, None])
        & (key_pos[None, :] >= 0)
    )
    kv_heads = query_heads.shape[1]

    def update(current):
        old_max, old_total, old_sum = current
        key_heads = block_of_keys.reshape(block_of_keys.shape[0], kv_heads, HEAD_SIZE)
        value_heads = block_of_values.reshape(block_of_values.shape[0], kv_heads, HEAD_SIZE)
        scores = jnp.einsum(
            "qhgd,khd->hgqk", query_heads, key_heads, preferred_element_type=jnp.float32
        ) * (1.0 / math.sqrt(HEAD_SIZE))
        masked = jnp.where(allowed[None, None], scores, -1e30)
        new_max = jnp.maximum(old_max, jnp.max(masked, axis=-1))
        weights = jnp.where(allowed[None, None], jnp.exp(masked - new_max[..., None]), 0.0)
        rescale = jnp.exp(old_max - new_max)
        new_total = old_total * rescale + jnp.sum(weights, axis=-1)
        new_sum = old_sum * rescale[..., None] + jnp.einsum(
            "hgqk,khd->hgqd",
            weights.astype(jnp.bfloat16),
            value_heads,
            preferred_element_type=jnp.float32,
        )
        return (new_max, new_total, new_sum)

    return lax.cond(jnp.any(allowed), update, lambda current: current, running)


def finish(running, row_count):
    summed = running[2] / running[1][..., None]
    return jnp.transpose(summed, (2, 0, 1, 3)).reshape(row_count, -1).astype(jnp.bfloat16)


def local(queries, key_vector_rows, values, doc_lengths):
    row_count = queries.shape[0]
    head_count = queries.shape[1] // HEAD_SIZE
    kv_heads = key_vector_rows.shape[1] // HEAD_SIZE
    query_group_width = head_count // kv_heads
    own_index = lax.axis_index("ctx")
    doc_ends = jnp.cumsum(doc_lengths)
    block_first = own_index * row_count
    local_pos = block_first + jnp.arange(row_count, dtype=jnp.int32)
    initial = (
        jnp.full((kv_heads, query_group_width, row_count), -1e30, jnp.float32),
        jnp.zeros((kv_heads, query_group_width, row_count), jnp.float32),
        jnp.zeros((kv_heads, query_group_width, row_count, HEAD_SIZE), jnp.float32),
    )
    query_info = (
        queries.reshape(row_count, kv_heads, query_group_width, HEAD_SIZE),
        local_pos,
        doc_numbers(doc_ends, local_pos),
        doc_ends,
    )
    piece_keys = lax.all_gather(key_vector_rows, "ctx", axis=0, tiled=True)
    piece_values = lax.all_gather(values, "ctx", axis=0, tiled=True)
    block_count = piece_keys.shape[0] // row_count

    def one_shard(shard_index, current):
        offset = shard_index * row_count
        block_of_keys = lax.dynamic_slice_in_dim(piece_keys, offset, row_count, 0)
        block_of_values = lax.dynamic_slice_in_dim(piece_values, offset, row_count, 0)
        key_pos = offset + jnp.arange(row_count, dtype=jnp.int32)
        return attend(current, block_of_keys, block_of_values, key_pos, query_info)

    running = lax.fori_loop(0, block_count, one_shard, initial)
    output = finish(running, row_count)
    return lax.all_to_all(output, "head", split_axis=0, concat_axis=1, tiled=True)


def solution(mesh):
    in_specs = (P("ctx", "head"), P("ctx", "head"), P("ctx", "head"), P())
    out_specs = P(("ctx", "head"), None)
    return jax.shard_map(local, mesh=mesh, in_specs=in_specs, out_specs=out_specs, check_vma=False)
```

profile of v0, /device:TPU:88, one launch (start us, length us, event | category | flops | bytes accessed | tf_op | source)
XLA Modules:
  0.0 454.3 jit_solution(7774628474176715688)
XLA Ops:
  10.6 117.2 %all-gather.3.cloned.1.call-done = bf16[8192,128]{1,0:T(8,128)(2,1)} async-done(((bf16[128,128]{1,0:T(8,128)(2,1)}), bf16[8192,128]{1,0:T(8,128)(2,1)}) %all-gather.3.cloned.1.call-update) | async-done | bytes 2097168 | tf_op jit(solution)/shard_map/all_gather | solution.py:72
  127.7 118.2 %all-gather.5.cloned.1.call-done = bf16[8192,128]{1,0:T(8,128)(2,1)} async-done(((bf16[128,128]{1,0:T(8,128)(2,1)}), bf16[8192,128]{1,0:T(8,128)(2,1)}) %all-gather.5.cloned.1.call-update) | async-done | bytes 2097168 | tf_op jit(solution)/shard_map/all_gather | solution.py:73
  246.0 181.0 %while.18 = (s32[]{:T(128)}, f32[1,8,128]{2,1,0:T(8,128)S(1)}, f32[1,8,128]{2,1,0:T(8,128)S(1)}, f32[1,8,128,128]{3,2,1,0:T(8,128)S(1)}, s32[128]{0:T(128)S(1)},...) while((s32[]{:T(128)}, f32[1,8,128]{2,1,0:T(8,128)S(1)}, ...), condition=%wide.region_9.10_spmd.clone, body=%wide.region_2.9_spmd.clone.sunk | while | flops 68685184 | bytes 3085365 | solution.py:83
  274.2 2.4 conditional.3
  278.1 2.4 conditional.3
  282.0 2.4 conditional.3
  283.1 1.2 fusion.3
  286.0 2.4 conditional.3
  289.9 2.4 conditional.3
  291.0 1.2 fusion.3
  293.9 2.4 conditional.3
  294.9 1.2 fusion.3
  297.8 2.4 conditional.3
  301.7 2.4 conditional.3
  302.8 1.2 fusion.3
  305.7 2.4 conditional.3
  309.6 2.4 conditional.3
  313.6 2.4 conditional.3
  314.6 1.2 fusion.3
  317.5 2.4 conditional.3
  321.4 2.4 conditional.3
  322.5 1.2 fusion.3
  325.4 2.4 conditional.3
  326.4 1.2 fusion.3
  329.3 2.4 conditional.3
  333.3 2.4 conditional.3
  334.3 1.2 fusion.3
  337.2 2.4 conditional.3
  341.1 2.4 conditional.3
  345.1 2.4 conditional.3
  346.1 1.2 fusion.3
  349.0 2.4 conditional.3
  353.0 2.4 conditional.3
  356.9 2.4 conditional.3
  358.0 1.2 fusion.3
  360.9 2.4 conditional.3
  364.8 2.4 conditional.3
  368.7 2.4 conditional.3
  372.7 2.4 conditional.3
  376.6 2.4 conditional.3
  380.6 2.4 conditional.3
  384.5 2.4 conditional.3
  388.4 2.4 conditional.3
  392.4 2.4 conditional.3
  396.3 2.4 conditional.3
  400.3 2.4 conditional.3
  404.2 2.4 conditional.3
  427.5 19.3 %all_to_all.16 = bf16[8,16,1024]{2,1,0:T(8,128)(2,1)S(1)} all-to-all(bf16[8,16,1024]{2,1,0:T(8,128)(2,1)S(1)} %convert_element_type.36), channel_id=1, replica_groups=mesh['ctx'=64,'head'=8] {'head'}, dimensions={0} | all-to-all | bytes 524288 | tf_op jit(solution)/shard_map/all_to_all | solution.py:85
  (498 shorter events, 132.6 us)
Async XLA Ops:
  6.5 121.2 %all-gather.3.cloned.1.call-start = ((), (), s32[]{:S(2)}) async-start(), calls=%async_computation.1 | async-start | bytes 2129920 | tf_op jit(solution)/shard_map/all_gather | solution.py:72
  7.3 238.7 %all-gather.5.cloned.1.call-start = ((), (), s32[]{:S(2)}) async-start(), calls=%async_computation.2 | async-start | bytes 2129920 | tf_op jit(solution)/shard_map/all_gather | solution.py:73
Sparse Core Ops, SparseCore 0:
  9.5 118.1 all-gather.2
  129.9 116.0 all-gather.4
where the time goes:
time: 460 us; the launch traced here: 454 us
  waiting for transfers between devices  237 us (52%)
  matrix products  74.8 us (16%)
  other arithmetic  64.7 us (14%)
  loops' own time  42 us (9%)
  blocking collectives  19.3 us (4%)
  between operations  13.5 us (3%)
    all_gather x1, waiting for transfers between devices, local(): piece_values = lax.all_gather(values, 'ctx', axis=0, tiled=True)  118 us
    all_gather x1, waiting for transfers between devices, local(): piece_keys = lax.all_gather(key_vector_rows, 'ctx', axis=0, tiled=True)  117 us
    reduce_or x64, other arithmetic, attend(): return lax.cond(jnp.any(allowed), update, lambda current: current, running)  48.3 us
    dot_general x34, matrix products, update(): jnp.einsum('hgqk,khd->hgqd', weights.astype(jnp.bfloat16), value_heads, p...  40.7 us
    another operation x1, loops' own time, local(): running = lax.fori_loop(0, block_count, one_shard, initial)  39.5 us
    dot_general x34, matrix products, update(): jnp.einsum('qhgd,khd->hgqk', query_heads, key_heads, preferred_element_ty...  34.1 us
    all_to_all x1, blocking collectives, local(): lax.all_to_all(output, 'head', split_axis=0, concat_axis=1, tiled=True)  19.3 us
    reduce_sum x65, other arithmetic, doc_numbers(): jnp.sum((doc_ends[None, :] <= positions[:, None]).astype(jnp.int32), axis=1)  11.1 us
  transfers between devices with their start and end apart: 2, of which 2 were waited for; matrix products, arithmetic and copies ran while one was open for 1% of the time, Pallas kernels for 0%

commit v1 on v0

--- a/solution.py
+++ b/solution.py
@@ -69,7 +69,9 @@
         doc_numbers(doc_ends, local_pos),
         doc_ends,
     )
-    piece_keys = lax.all_gather(key_vector_rows, "ctx", axis=0, tiled=True)
+    piece_keys = jnp.concatenate(
+        lax.all_to_all(jnp.stack([key_vector_rows] * lax.axis_size("ctx")), "ctx", 0, 0), axis=0
+    )
     piece_values = lax.all_gather(values, "ctx", axis=0, tiled=True)
     block_count = piece_keys.shape[0] // row_count
 

time: 460 us -> 352 us (0.77)
  the two profiles are of different devices: /device:TPU:88 before, /device:TPU:25 now
where the time goes in v1:
time: 352 us; the launch traced here: 349 us
  waiting for transfers between devices  140 us (40%)
  other arithmetic  65.4 us (19%)
  matrix products  47.5 us (13%)
  loops' own time  45.1 us (13%)
  blocking collectives  18.5 us (5%)
  starting transfers between devices  14.8 us (4%)
  between operations  13.5 us (4%)
  local copies, waits for them, and re-layouts  4.17 us (1%)
    all_gather x1, waiting for transfers between devices, local(): piece_values = lax.all_gather(values, 'ctx', axis=0, tiled=True)  87 us
    all_to_all x1, waiting for transfers between devices, local(): lax.all_to_all(jnp.stack([key_vector_rows] * lax.axis_size('ctx')), 'ctx'...  52.3 us
    reduce_or x64, other arithmetic, attend(): return lax.cond(jnp.any(allowed), update, lambda current: current, running)  48.9 us
    another operation x1, loops' own time, local(): running = lax.fori_loop(0, block_count, one_shard, initial)  42.7 us
    dot_general x33, matrix products, update(): jnp.einsum('hgqk,khd->hgqd', weights.astype(jnp.bfloat16), value_heads, p...  39.4 us
    all_to_all x1, blocking collectives, local(): lax.all_to_all(output, 'head', split_axis=0, concat_axis=1, tiled=True)  18.5 us
    all_to_all x1, starting transfers between devices, local(): lax.all_to_all(jnp.stack([key_vector_rows] * lax.axis_size('ctx')), 'ctx'...  14.8 us
    reduce_sum x65, other arithmetic, doc_numbers(): jnp.sum((doc_ends[None, :] <= positions[:, None]).astype(jnp.int32), axis=1)  11.1 us
  transfers between devices with their start and end apart: 2, of which 2 were waited for; matrix products, arithmetic and copies ran while one was open for 0% of the time, Pallas kernels for 0%

profile of v1, /device:TPU:25, one launch (start us, length us, event | category | flops | bytes accessed | tf_op | source)
XLA Modules:
  0.0 349.0 jit_solution(10697316812104132786)
XLA Ops:
  6.5 2.6 stack.2
  9.1 14.8 %all-to-all-start = ((bf16[64,128,128]{2,1,0:T(8,128)(2,1)}), bf16[64,128,128]{2,1,0:T(8,128)(2,1)S(1)}, u32[]{:S(2)}, u32[]{:S(2)}) async-start(bf16[64,128,128]{2,1,0:T(8,128)(2,1)} %stack.2), calls=%async_computation | async-start | bytes 4194304 | tf_op jit(solution)/shard_map/all_to_all | solution.py:73
  25.6 52.3 %all-to-all-done = bf16[64,128,128]{2,1,0:T(8,128)(2,1)S(1)} async-done(((bf16[64,128,128]{2,1,0:T(8,128)(2,1)}), bf16[64,128,128]{2,1,0:T(8,128)(2,1)S(1)}, u32[]{:S(2)}, u32[]{:S(2)}) %all-to-all-start) | async-done | bytes 2097184 | tf_op jit(solution)/shard_map/all_to_all | solution.py:73
  77.9 87.0 %all-gather.2.cloned.1.call-done = bf16[8192,128]{1,0:T(8,128)(2,1)} async-done(((bf16[128,128]{1,0:T(8,128)(2,1)}), bf16[8192,128]{1,0:T(8,128)(2,1)}) %all-gather.2.cloned.1.call-update) | async-done | bytes 2097168 | tf_op jit(solution)/shard_map/all_gather | solution.py:75
  164.9 157.4 %while.18 = (s32[]{:T(128)}, f32[1,8,128]{2,1,0:T(8,128)S(1)}, f32[1,8,128]{2,1,0:T(8,128)S(1)}, f32[1,8,128,128]{3,2,1,0:T(8,128)S(1)}, s32[128]{0:T(128)S(1)},...) while((s32[]{:T(128)}, f32[1,8,128]{2,1,0:T(8,128)S(1)}, ...), condition=%wide.region_9.10_spmd.clone, body=%wide.region_2.9_spmd.clone.sunk | while | flops 68685184 | bytes 3085365 | solution.py:85
  194.2 1.6 conditional.3
  194.5 1.2 fusion.3
  197.5 1.6 conditional.3
  197.8 1.2 fusion.3
  200.7 1.6 conditional.3
  201.0 1.2 fusion.3
  203.9 1.6 conditional.3
  204.2 1.2 fusion.3
  207.2 1.6 conditional.3
  207.5 1.2 fusion.3
  210.4 1.6 conditional.3
  210.7 1.2 fusion.3
  213.7 1.6 conditional.3
  214.0 1.2 fusion.3
  216.9 1.6 conditional.3
  217.2 1.2 fusion.3
  220.2 1.6 conditional.3
  223.4 1.6 conditional.3
  223.7 1.2 fusion.3
  226.6 1.6 conditional.3
  229.9 1.6 conditional.3
  233.1 1.6 conditional.3
  236.4 1.6 conditional.3
  239.6 1.6 conditional.3
  242.9 1.6 conditional.3
  246.1 1.6 conditional.3
  249.3 1.6 conditional.3
  252.6 1.6 conditional.3
  255.8 1.6 conditional.3
  259.1 1.6 conditional.3
  262.3 1.6 conditional.3
  265.5 1.6 conditional.3
  268.8 1.6 conditional.3
  272.0 1.6 conditional.3
  275.3 1.6 conditional.3
  278.5 1.6 conditional.3
  281.8 1.6 conditional.3
  285.0 1.6 conditional.3
  288.2 1.6 conditional.3
  291.5 1.6 conditional.3
  294.7 1.6 conditional.3
  298.0 1.6 conditional.3
  322.9 18.5 %all_to_all.21 = bf16[8,16,1024]{2,1,0:T(8,128)(2,1)S(1)} all-to-all(bf16[8,16,1024]{2,1,0:T(8,128)(2,1)S(1)} %convert_element_type.36), channel_id=1, replica_groups=mesh['ctx'=64,'head'=8] {'head'}, dimensions={0} | all-to-all | bytes 524288 | tf_op jit(solution)/shard_map/all_to_all | solution.py:87
  (496 shorter events, 104.8 us)
Async XLA Ops:
  9.1 15.5 %copy-start.1 = (s32[128]{0:T(128)S(1)}, s32[128]{0:T(128)}, u32[]{:S(2)}) copy-start(s32[128]{0:T(128)} %param.11) | copy-start | bytes 1540
  9.1 15.9 %copy-start = (bf16[128,1024]{1,0:T(8,128)(2,1)S(1)}, bf16[128,1024]{1,0:T(8,128)(2,1)}, u32[]{:S(2)}) copy-start(bf16[128,1024]{1,0:T(8,128)(2,1)} %param.8) | copy-start | bytes 786436
  9.1 68.8 %all-to-all-start = ((bf16[64,128,128]{2,1,0:T(8,128)(2,1)}), bf16[64,128,128]{2,1,0:T(8,128)(2,1)S(1)}, u32[]{:S(2)}, u32[]{:S(2)}) async-start(bf16[64,128,128]{2,1,0:T(8,128)(2,1)} %stack.2), calls=%async_computation | async-start | bytes 4194304 | tf_op jit(solution)/shard_map/all_to_all | solution.py:73
  23.9 141.0 %all-gather.2.cloned.1.call-start = ((), (), s32[]{:S(2)}) async-start(), calls=%async_computation.2 | async-start | bytes 2129920 | tf_op jit(solution)/shard_map/all_gather | solution.py:75
Sparse Core Ops, SparseCore 0:
  26.9 137.9 all-gather.1
